TPU v7x, 32 devices: a whole 2x2x4 slice. The times are simulated.
32 devices in a mesh: slab: 2 (over x), brick: 16 (over z, y, core).
Axes of the slice: x: 2, y: 2, z: 4, core: 2. Of those that a mesh axis runs over, the one named last changes fastest.
Arguments:
- features: bfloat16 [64, 64, 512], P(('slab', 'brick')), may hold values from -6 to 6
- weight: bfloat16 [27, 64, 64], replicated, may hold values from -0.15625 to 0.15625
- cotangent: bfloat16 [64, 64, 512], P(('slab', 'brick')), may hold values from -6 to 6
- occupancy: int32 [64, 24], P(('slab', 'brick')), may hold values from 0 to 4194303, as said below
- neighbours: int32 [64, 27], P(('slab', 'brick')), may hold values from -1 to 63, as said below
Outputs:
- output: bfloat16 [64, 64, 512], P(('slab', 'brick'))
- grad_input: bfloat16 [64, 64, 512], P(('slab', 'brick'))
- grad_weight: float32 [27, 64, 64], replicated
Inputs may be any that keep to these rules, and one draw needn't show every extreme that they name: `neighbours`: slot j of the device at (slab s, brick t), that is slot (16 s + t) * 2 + j, holds the brick of z layer 2 s + j and column t along x, at some row y; slot 0 of every device holds a brick, the others may be absent. For offset k = 9 (a + 1) + 3 (c + 1) + (e + 1), the entry of a present slot is the slot that holds the brick at layer 2 s + j + a, row y + c, column t + e if that brick is present, else -1; an absent slot's entries are all -1. The lists are symmetric, and the middle entry of a present slot is the slot itself. Bit j of word w of a slot is the occupancy of voxel 22 w + j; bits from voxel 512 on are zero. Absent slots are wholly unoccupied; slot 0 is fully occupied.
All inputs are finite; a program needn't handle non-finite values.
Results may differ from a plain program's by a relative error of at most 0.001.
Values may be sent and summed in bfloat16 or wider, within the bound.
A program may use at most 64 MiB of HBM per device.

v0:
```python
import math
import jax
import jax.numpy as jnp
from jax import lax
from jax.sharding import PartitionSpec as P

EDGE = 8


def extended(block, sides, width):
    for axis, dim in sides:
        count = lax.axis_size(axis)
        forward = [(i, i + 1) for i in range(count - 1)]
        backward = [(target, source) for source, target in forward]
        low = lax.ppermute(
            lax.slice_in_dim(block, block.shape[dim] - width, None, axis=dim), axis, forward
        )
        high = lax.ppermute(lax.slice_in_dim(block, 0, width, axis=dim), axis, backward)
        block = jnp.concatenate([low, block, high], axis=dim)
    return block


def unpack_bits(packed, voxels):
    places = jnp.arange(22, dtype=jnp.int32)
    bit_table = jnp.bitwise_and(jnp.right_shift(packed[..., :, None], places), 1)
    return bit_table.reshape(packed.shape[:-1] + (packed.shape[-1] * 22,))[..., :voxels]


def cut(length, side):
    if side < 0:
        return slice(length - 1, length)
    if side > 0:
        return slice(0, 1)
    return slice(0, length)


def windows(padded, direction):
    channels = padded.shape[0]
    pieces = []
    for shift_z in (-1, 0, 1):
        for shift_y in (-1, 0, 1):
            for shift_x in (-1, 0, 1):
                begin_z = 1 + direction * shift_z
                begin_y = 1 + direction * shift_y
                begin_x = 1 + direction * shift_x
                window = padded[
                    :, begin_z : begin_z + EDGE, begin_y : begin_y + EDGE, begin_x : begin_x + EDGE
                ]
                pieces.append(window.reshape(channels, EDGE * EDGE * EDGE))
    return jnp.stack(pieces, 0).reshape(27 * channels, EDGE * EDGE * EDGE)


def first_row(face):
    return face.reshape(face.shape[0], EDGE, EDGE)[:, 0, :]


def last_row(face):
    return face.reshape(face.shape[0], EDGE, EDGE)[:, EDGE - 1, :]


def per_device(features, weight, cotangent, occupancy, neighbours):
    slots = features.shape[0]
    channels = features.shape[1]
    voxels = features.shape[2]
    width = 2 * channels
    face_size = EDGE * EDGE
    occupied = unpack_bits(occupancy, voxels).astype(jnp.bfloat16)
    masked_input = features * occupied[:, None, :]
    masked_grad = cotangent * occupied[:, None, :]
    cube = jnp.concatenate([masked_input, masked_grad], 1).reshape(slots, width, EDGE, EDGE, EDGE)
    present = (neighbours >= 0).astype(jnp.bfloat16)
    low_x = cube[..., 0].reshape(slots, width, face_size)
    high_x = cube[..., EDGE - 1].reshape(slots, width, face_size)
    low_z = cube[0, :, 0].reshape(width, face_size)
    high_z = cube[slots - 1, :, EDGE - 1].reshape(width, face_size)
    payload = jnp.concatenate([low_x, high_x, low_z[None], high_z[None]], 0)
    beside_all = extended(payload[None, None], (("slab", 0), ("brick", 1)), 1)
    right_faces = beside_all[1, 2, :slots]
    left_faces = beside_all[1, 0, slots : 2 * slots]
    above_face = beside_all[2, 1, 2 * slots]
    below_face = beside_all[0, 1, 2 * slots + 1]
    above_right = first_row(beside_all[2, 2, 0])
    above_left = first_row(beside_all[2, 0, slots])
    below_right = last_row(beside_all[0, 2, slots - 1])
    below_left = last_row(beside_all[0, 0, 2 * slots - 1])

    def piece(slot, shift_z, shift_y, shift_x):
        target = slot + shift_z
        offset = 9 * (shift_z + 1) + 3 * (shift_y + 1) + (shift_x + 1)
        span_z = cut(EDGE, shift_z)
        span_y = cut(EDGE, shift_y)
        if 0 <= target < slots:
            if shift_x == 0:
                block = cube[target][:, span_z, span_y, :]
            else:
                source = right_faces if shift_x == 1 else left_faces
                block = source[target].reshape(width, EDGE, EDGE)[:, span_z, span_y][..., None]
        elif target >= slots:
            if shift_x == 0:
                block = above_face.reshape(width, EDGE, EDGE)[:, None, span_y, :]
            else:
                edge_row = above_right if shift_x == 1 else above_left
                block = edge_row[:, None, span_y, None]
        elif shift_x == 0:
            block = below_face.reshape(width, EDGE, EDGE)[:, None, span_y, :]
        else:
            edge_row = below_right if shift_x == 1 else below_left
            block = edge_row[:, None, span_y, None]
        return block * present[slot, offset]

    forward_matrix = jnp.transpose(weight, (1, 0, 2)).reshape(channels, 27 * channels)
    backward_matrix = jnp.transpose(weight, (2, 0, 1)).reshape(channels, 27 * channels)
    outputs = []
    gradients = []
    local_terms = jnp.zeros((channels, 27 * channels), jnp.float32)
    for slot in range(slots):
        layers = []
        for shift_z in (-1, 0, 1):
            rows = []
            for shift_y in (-1, 0, 1):
                columns = [piece(slot, shift_z, shift_y, shift_x) for shift_x in (-1, 0, 1)]
                rows.append(jnp.concatenate(columns, 3))
            layers.append(jnp.concatenate(rows, 2))
        padded = jnp.concatenate(layers, 1)
        scaling = occupied[slot].astype(jnp.float32)[None, :]
        input_patches = windows(padded[:channels], 1)
        output_rows = jnp.dot(forward_matrix, input_patches, preferred_element_type=jnp.float32)
        outputs.append((output_rows * scaling).astype(jnp.bfloat16))
        local_terms = local_terms + lax.dot_general(
            masked_grad[slot],
            input_patches,
            (((1,), (1,)), ((), ())),
            preferred_element_type=jnp.float32,
        )
        grad_patches = windows(padded[channels:], -1)
        grad_rows = jnp.dot(backward_matrix, grad_patches, preferred_element_type=jnp.float32)
        gradients.append((grad_rows * scaling).astype(jnp.bfloat16))
    total = lax.psum(local_terms, ("slab", "brick"))
    slot_count = slots * lax.axis_size("slab") * lax.axis_size("brick")
    grad_weight = jnp.transpose(total.reshape(channels, 27, channels), (1, 0, 2)) / math.sqrt(
        voxels * slot_count
    )
    return (jnp.stack(outputs, 0), jnp.stack(gradients, 0), grad_weight)


def solution(mesh):
    placed = (
        P(("slab", "brick"), None, None),
        P(),
        P(("slab", "brick"), None, None),
        P(("slab", "brick"), None),
        P(("slab", "brick"), None),
    )
    return jax.shard_map(
        per_device,
        mesh=mesh,
        in_specs=placed,
        out_specs=(P(("slab", "brick"), None, None), P(("slab", "brick"), None, None), P()),
        check_vma=False,
    )
```

profile of v0, /device:TPU:1, one launch (start us, length us, event | category | flops | bytes accessed | tf_op | source)
XLA Modules:
  0.0 351.3 jit_solution(4987366351810817979)
XLA Ops:
  10.9 1.3 collective-permute-start.1
  12.2 4.0 %collective-permute-start = (bf16[1,1,6,128,64]{3,4,2,1,0:T(8,128)(2,1)S(1)}, bf16[1,1,6,128,64]{3,4,2,1,0:T(8,128)(2,1)S(1)}, u32[]{:S(2)}, u32[]{:S(2)}) collective-permute-start(bf16[1,1,6,128,64]{3,4,2,1,0:T(8,128)(2,1)S(1)} %maximum_bitcast_fusion), channel_id=1, source_target_pairs={{0,16},{1,17},{2,18},{3,19},{4,20},{5,21},{6,22},{7,23},{8,24},{9,... | collective-permute-start | bytes 294920 | tf_op jit(solution)/shard_map/ppermute | solution.py:15
  19.2 1.2 slice_multiply_fusion.3
  20.9 1.3 slice_multiply_fusion.2
  22.9 1.9 slice_multiply_fusion.19
  24.8 1.2 slice_multiply_fusion.1
  26.0 1.3 slice_multiply_fusion.5
  27.4 1.8 slice_multiply_fusion.15
  29.3 2.8 collective-permute-start.3
  32.1 4.2 %collective-permute-start.2 = (bf16[3,1,6,128,64]{3,4,2,1,0:T(8,128)(2,1)S(1)}, bf16[3,1,6,128,64]{3,4,2,1,0:T(8,128)(2,1)S(1)}, u32[]{:S(2)}, u32[]{:S(2)}) collective-permute-start(bf16[3,1,6,128,64]{3,4,2,1,0:T(8,128)(2,1)S(1)} %pad_maximum_fusion), channel_id=1, source_target_pairs={{0,1},{1,2},{2,3},{3,4},{4,5},{5,6},{6,7},{7,8},{8,9},{9,10},{10,1... | collective-permute-start | bytes 884744 | tf_op jit(solution)/shard_map/ppermute | solution.py:15
  36.3 1.2 multiply_bitcast_fusion
  38.7 1.8 fusion.28
  40.5 1.9 fusion.34
  42.4 1.2 slice_bitcast_fusion.6
  44.2 1.2 multiply_bitcast_fusion.8
  49.1 1.2 multiply_bitcast_fusion.6
  51.0 1.3 slice_bitcast_fusion.7
  56.2 1.3 multiply_bitcast_fusion.9
  58.0 1.2 multiply_bitcast_fusion.7
  69.4 1.6 copy.308
  71.0 1.6 copy.307
  72.7 1.6 copy.306
  74.3 1.6 copy.259
  96.5 1.3 multiply_bitcast_fusion.17
  111.3 2.0 fusion.45
  113.3 2.0 fusion.46
  115.6 1.6 fusion.48
  117.1 1.6 copy.277
  118.7 1.6 copy.276
  120.4 1.6 copy.275
  122.0 1.6 copy.274
  123.6 1.6 copy.273
  125.2 1.6 copy.272
  126.8 1.6 copy.271
  128.5 1.6 copy.270
  130.1 1.6 copy.269
  131.7 1.6 copy.229
  133.3 1.6 copy.228
  134.9 1.7 copy.227
  154.0 2.1 fusion.41
  156.1 1.9 fusion.42
  158.3 1.4 fusion.49
  159.8 1.6 copy.323
  161.4 1.6 copy.322
  174.0 1.2 multiply_bitcast_fusion.12
  175.3 1.2 multiply_bitcast_fusion.13
  176.8 1.6 fusion.50
  178.4 1.6 copy.305
  180.0 1.6 copy.304
  181.6 1.6 copy.303
  183.2 1.6 copy.302
  184.9 1.6 copy.301
  186.5 1.6 copy.300
  188.1 1.6 copy.299
  189.7 1.6 copy.298
  191.4 1.6 copy.297
  193.0 1.6 copy.268
  194.6 1.6 copy.267
  196.2 1.6 copy.266
  197.9 1.6 copy.265
  199.5 1.6 copy.264
  213.8 1.4 convolution_add_fusion
  219.3 122.2 %all-reduce.2.cloned.1.call-done = f32[64,1728]{1,0:T(8,128)} async-done(((f32[64,1728]{1,0:T(8,128)}), f32[64,1728]{1,0:T(8,128)}) %all-reduce.2.cloned.1.call-update) | async-done | bytes 442384 | tf_op jit(solution)/shard_map/psum | solution.py:138
  343.0 1.4 copy.325
  (543 shorter events, 107.7 us)
Async XLA Ops:
  7.2 143.5 %copy-start = (bf16[27,64,64]{2,1,0:T(8,128)(2,1)S(1)}, bf16[27,64,64]{2,1,0:T(8,128)(2,1)}, u32[]{:S(2)}) copy-start(bf16[27,64,64]{2,1,0:T(8,128)(2,1)} %param.6) | copy-start | bytes 663556
  7.2 9.0 %copy-start.138 = (s32[2,27]{1,0:T(2,128)S(1)}, s32[2,27]{1,0:T(2,128)}, u32[]{:S(2)}) copy-start(s32[2,27]{1,0:T(2,128)} %param.9) | copy-start | bytes 652
  7.2 334.3 %all-reduce.2.cloned.1.call-start = ((), (), s32[]{:S(2)}) async-start(), calls=%async_computation | async-start | bytes 917504 | tf_op jit(solution)/shard_map/psum | solution.py:138
  10.9 18.3 %collective-permute-start.1 = (bf16[1,1,6,128,64]{3,4,2,1,0:T(8,128)(2,1)S(1)}, bf16[1,1,6,128,64]{3,4,2,1,0:T(8,128)(2,1)S(1)}, u32[]{:S(2)}, u32[]{:S(2)}) collective-permute-start(bf16[1,1,6,128,64]{3,4,2,1,0:T(8,128)(2,1)S(1)} %maximum_bitcast_fusion), channel_id=1, source_target_pairs={{16,0},{17,1},{18,2},{19,3},{20,4},{21,5},{22,6},{23,7},{24,8},{25... | collective-permute-start | bytes 294920 | tf_op jit(solution)/shard_map/ppermute | solution.py:18
  12.2 17.0 %collective-permute-start = (bf16[1,1,6,128,64]{3,4,2,1,0:T(8,128)(2,1)S(1)}, bf16[1,1,6,128,64]{3,4,2,1,0:T(8,128)(2,1)S(1)}, u32[]{:S(2)}, u32[]{:S(2)}) collective-permute-start(bf16[1,1,6,128,64]{3,4,2,1,0:T(8,128)(2,1)S(1)} %maximum_bitcast_fusion), channel_id=1, source_target_pairs={{0,16},{1,17},{2,18},{3,19},{4,20},{5,21},{6,22},{7,23},{8,24},{9,... | collective-permute-start | bytes 294920 | tf_op jit(solution)/shard_map/ppermute | solution.py:15
  27.4 33.3 %copy-start.86 = (bf16[128,8,1,8]{0,3,2,1:T(8,128)(2,1)}, bf16[128,8,1,8]{0,3,2,1:T(8,128)(2,1)S(1)}, u32[]{:S(2)}) copy-start(bf16[128,8,1,8]{0,3,2,1:T(8,128)(2,1)S(1)} %get-tuple-element.145) | copy-start | bytes 49156
  27.4 33.3 %copy-start.88 = (bf16[128,8,1,8]{0,3,2,1:T(8,128)(2,1)}, bf16[128,8,1,8]{0,3,2,1:T(8,128)(2,1)S(1)}, u32[]{:S(2)}) copy-start(bf16[128,8,1,8]{0,3,2,1:T(8,128)(2,1)S(1)} %get-tuple-element.146) | copy-start | bytes 49156
  29.3 13.1 %collective-permute-start.3 = (bf16[3,1,6,128,64]{3,4,2,1,0:T(8,128)(2,1)S(1)}, bf16[3,1,6,128,64]{3,4,2,1,0:T(8,128)(2,1)S(1)}, u32[]{:S(2)}, u32[]{:S(2)}) collective-permute-start(bf16[3,1,6,128,64]{3,4,2,1,0:T(8,128)(2,1)S(1)} %pad_maximum_fusion), channel_id=1, source_target_pairs={{1,0},{2,1},{3,2},{4,3},{5,4},{6,5},{7,6},{8,7},{9,8},{10,9},{11,1... | collective-permute-start | bytes 884744 | tf_op jit(solution)/shard_map/ppermute | solution.py:18
  32.1 18.9 %collective-permute-start.2 = (bf16[3,1,6,128,64]{3,4,2,1,0:T(8,128)(2,1)S(1)}, bf16[3,1,6,128,64]{3,4,2,1,0:T(8,128)(2,1)S(1)}, u32[]{:S(2)}, u32[]{:S(2)}) collective-permute-start(bf16[3,1,6,128,64]{3,4,2,1,0:T(8,128)(2,1)S(1)} %pad_maximum_fusion), channel_id=1, source_target_pairs={{0,1},{1,2},{2,3},{3,4},{4,5},{5,6},{6,7},{7,8},{8,9},{9,10},{10,1... | collective-permute-start | bytes 884744 | tf_op jit(solution)/shard_map/ppermute | solution.py:15
  43.6 21.7 %copy-start.116 = (bf16[128,8,8]{0,2,1:T(8,128)(2,1)}, bf16[128,8,8]{0,2,1:T(8,128)(2,1)S(1)}, u32[]{:S(2)}) copy-start(bf16[128,8,8]{0,2,1:T(8,128)(2,1)S(1)} %get-tuple-element.117) | copy-start | bytes 49156
  47.3 13.4 %copy-start.102 = (bf16[128,8,1,1]{0,3,2,1:T(2,128)(2,1)}, bf16[128,8,1,1]{0,3,2,1:T(2,128)(2,1)S(1)}, u32[]{:S(2)}) copy-start(bf16[128,8,1,1]{0,3,2,1:T(2,128)(2,1)S(1)} %copy.198) | copy-start | bytes 6148
  47.3 13.4 %copy-start.104 = (bf16[128,8,1,1]{0,3,2,1:T(2,128)(2,1)}, bf16[128,8,1,1]{0,3,2,1:T(2,128)(2,1)S(1)}, u32[]{:S(2)}) copy-start(bf16[128,8,1,1]{0,3,2,1:T(2,128)(2,1)S(1)} %copy.192) | copy-start | bytes 6148
  52.4 14.2 %copy-start.117 = (bf16[128,8,8]{0,2,1:T(8,128)(2,1)}, bf16[128,8,8]{0,2,1:T(8,128)(2,1)S(1)}, u32[]{:S(2)}) copy-start(bf16[128,8,8]{0,2,1:T(8,128)(2,1)S(1)} %get-tuple-element.111) | copy-start | bytes 49156
  87.7 8.8 %copy-start.137 = (bf16[128,8]{0,1:T(8,128)(2,1)S(1)}, bf16[128,8]{0,1:T(8,128)(2,1)}, u32[]{:S(2)}) copy-start(bf16[128,8]{0,1:T(8,128)(2,1)} %get-tuple-element.162) | copy-start | bytes 6148
  87.7 10.1 %copy-start.87 = (bf16[128,8,1,8]{0,3,2,1:T(8,128)(2,1)S(1)}, bf16[128,8,1,8]{0,3,2,1:T(8,128)(2,1)}, u32[]{:S(2)}) copy-start(bf16[128,8,1,8]{0,3,2,1:T(8,128)(2,1)} %copy-done.86) | copy-start | bytes 49156
  87.7 10.1 %copy-start.89 = (bf16[128,8,1,8]{0,3,2,1:T(8,128)(2,1)S(1)}, bf16[128,8,1,8]{0,3,2,1:T(8,128)(2,1)}, u32[]{:S(2)}) copy-start(bf16[128,8,1,8]{0,3,2,1:T(8,128)(2,1)} %copy-done.88) | copy-start | bytes 49156
  87.7 10.1 %copy-start.103 = (bf16[128,8,1,1]{0,3,2,1:T(2,128)(2,1)S(1)}, bf16[128,8,1,1]{0,3,2,1:T(2,128)(2,1)}, u32[]{:S(2)}) copy-start(bf16[128,8,1,1]{0,3,2,1:T(2,128)(2,1)} %copy-done.102) | copy-start | bytes 6148
  87.8 10.1 %copy-start.105 = (bf16[128,8,1,1]{0,3,2,1:T(2,128)(2,1)S(1)}, bf16[128,8,1,1]{0,3,2,1:T(2,128)(2,1)}, u32[]{:S(2)}) copy-start(bf16[128,8,1,1]{0,3,2,1:T(2,128)(2,1)} %copy-done.104) | copy-start | bytes 6148
  87.8 10.1 %copy-start.107 = (bf16[128,8,1,1]{0,3,2,1:T(2,128)(2,1)S(1)}, bf16[128,8,1,1]{0,3,2,1:T(2,128)(2,1)}, u32[]{:S(2)}) copy-start(bf16[128,8,1,1]{0,3,2,1:T(2,128)(2,1)} %copy-done.106) | copy-start | bytes 6148
  87.8 10.1 %copy-start.109 = (bf16[128,8,1,1]{0,3,2,1:T(2,128)(2,1)S(1)}, bf16[128,8,1,1]{0,3,2,1:T(2,128)(2,1)}, u32[]{:S(2)}) copy-start(bf16[128,8,1,1]{0,3,2,1:T(2,128)(2,1)} %copy-done.108) | copy-start | bytes 6148
  87.8 10.1 %copy-start.111 = (bf16[128,1,8,8]{0,3,2,1:T(8,128)(2,1)S(1)}, bf16[128,1,8,8]{0,3,2,1:T(8,128)(2,1)}, u32[]{:S(2)}) copy-start(bf16[128,1,8,8]{0,3,2,1:T(8,128)(2,1)} %get-tuple-element.151) | copy-start | bytes 49156
  87.8 10.1 %copy-start.124 = (bf16[128,1,8,1]{0,3,2,1:T(2,128)(2,1)S(1)}, bf16[128,1,8,1]{0,3,2,1:T(2,128)(2,1)}, u32[]{:S(2)}) copy-start(bf16[128,1,8,1]{0,3,2,1:T(2,128)(2,1)} %copy.188) | copy-start | bytes 6148
  87.8 10.1 %copy-start.125 = (bf16[128,1,8,1]{0,3,2,1:T(2,128)(2,1)S(1)}, bf16[128,1,8,1]{0,3,2,1:T(2,128)(2,1)}, u32[]{:S(2)}) copy-start(bf16[128,1,8,1]{0,3,2,1:T(2,128)(2,1)} %copy.187) | copy-start | bytes 6148
  87.8 10.1 %copy-start.132 = (bf16[128,1,1,8]{0,3,2,1:T(8,128)(2,1)S(1)}, bf16[128,1,1,8]{0,3,2,1:T(8,128)(2,1)}, u32[]{:S(2)}) copy-start(bf16[128,1,1,8]{0,3,2,1:T(8,128)(2,1)} %get-tuple-element.159) | copy-start | bytes 6148
  87.8 10.1 %copy-start.133 = (bf16[128,1,1,8]{0,3,2,1:T(8,128)(2,1)S(1)}, bf16[128,1,1,8]{0,3,2,1:T(8,128)(2,1)}, u32[]{:S(2)}) copy-start(bf16[128,1,1,8]{0,3,2,1:T(8,128)(2,1)} %get-tuple-element.160) | copy-start | bytes 6148
  99.5 15.7 %copy-start.113 = (bf16[128,1,8,8]{0,3,2,1:T(8,128)(2,1)S(1)}, bf16[128,1,8,8]{0,3,2,1:T(8,128)(2,1)}, u32[]{:S(2)}) copy-start(bf16[128,1,8,8]{0,3,2,1:T(8,128)(2,1)} %slice_multiply_fusion.3) | copy-start | bytes 49156
  99.5 15.7 %copy-start.122 = (bf16[128,1,8,1]{0,3,2,1:T(2,128)(2,1)S(1)}, bf16[128,1,8,1]{0,3,2,1:T(2,128)(2,1)}, u32[]{:S(2)}) copy-start(bf16[128,1,8,1]{0,3,2,1:T(2,128)(2,1)} %copy.202) | copy-start | bytes 6148
  99.5 15.7 %copy-start.123 = (bf16[128,1,8,1]{0,3,2,1:T(2,128)(2,1)S(1)}, bf16[128,1,8,1]{0,3,2,1:T(2,128)(2,1)}, u32[]{:S(2)}) copy-start(bf16[128,1,8,1]{0,3,2,1:T(2,128)(2,1)} %copy.201) | copy-start | bytes 6148
  99.6 15.7 %copy-start.130 = (bf16[128,1,1,8]{0,3,2,1:T(8,128)(2,1)S(1)}, bf16[128,1,1,8]{0,3,2,1:T(8,128)(2,1)}, u32[]{:S(2)}) copy-start(bf16[128,1,1,8]{0,3,2,1:T(8,128)(2,1)} %get-tuple-element.143) | copy-start | bytes 6148
  99.6 15.8 %copy-start.131 = (bf16[128,1,1,8]{0,3,2,1:T(8,128)(2,1)S(1)}, bf16[128,1,1,8]{0,3,2,1:T(8,128)(2,1)}, u32[]{:S(2)}) copy-start(bf16[128,1,1,8]{0,3,2,1:T(8,128)(2,1)} %get-tuple-element.144) | copy-start | bytes 6148
  134.9 14.7 %copy-start.20 = (bf16[1,64,512]{2,1,0:T(8,128)(2,1)S(1)}, bf16[1,64,512]{2,1,0:T(8,128)(2,1)}, u32[]{:S(2)}) copy-start(bf16[1,64,512]{2,1,0:T(8,128)(2,1)} %copy.220) | copy-start | bytes 196612
  137.3 12.2 %copy-start.24 = (bf16[1,64,512]{2,1,0:T(8,128)(2,1)S(1)}, bf16[1,64,512]{2,1,0:T(8,128)(2,1)}, u32[]{:S(2)}) copy-start(bf16[1,64,512]{2,1,0:T(8,128)(2,1)} %copy.218) | copy-start | bytes 196612
  137.3 12.3 %copy-start.23 = (bf16[1,64,512]{2,1,0:T(8,128)(2,1)S(1)}, bf16[1,64,512]{2,1,0:T(8,128)(2,1)}, u32[]{:S(2)}) copy-start(bf16[1,64,512]{2,1,0:T(8,128)(2,1)} %copy.219) | copy-start | bytes 196612
  138.0 11.4 %copy-start.42 = (bf16[1,64,512]{2,1,0:T(8,128)(2,1)S(1)}, bf16[1,64,512]{2,1,0:T(8,128)(2,1)}, u32[]{:S(2)}) copy-start(bf16[1,64,512]{2,1,0:T(8,128)(2,1)} %copy.215) | copy-start | bytes 196612
  138.0 11.5 %copy-start.39 = (bf16[1,64,512]{2,1,0:T(8,128)(2,1)S(1)}, bf16[1,64,512]{2,1,0:T(8,128)(2,1)}, u32[]{:S(2)}) copy-start(bf16[1,64,512]{2,1,0:T(8,128)(2,1)} %copy.217) | copy-start | bytes 196612
  138.8 10.7 %copy-start.49 = (bf16[1,64,512]{2,1,0:T(8,128)(2,1)S(1)}, bf16[1,64,512]{2,1,0:T(8,128)(2,1)}, u32[]{:S(2)}) copy-start(bf16[1,64,512]{2,1,0:T(8,128)(2,1)} %copy.214) | copy-start | bytes 196612
  138.8 10.7 %copy-start.45 = (bf16[1,64,512]{2,1,0:T(8,128)(2,1)S(1)}, bf16[1,64,512]{2,1,0:T(8,128)(2,1)}, u32[]{:S(2)}) copy-start(bf16[1,64,512]{2,1,0:T(8,128)(2,1)} %copy.216) | copy-start | bytes 196612
  139.5 10.3 %copy-start.72 = (bf16[1,64,512]{2,1,0:T(8,128)(2,1)S(1)}, bf16[1,64,512]{2,1,0:T(8,128)(2,1)}, u32[]{:S(2)}) copy-start(bf16[1,64,512]{2,1,0:T(8,128)(2,1)} %copy.227) | copy-start | bytes 196612
  139.5 10.3 %copy-start.70 = (bf16[1,64,512]{2,1,0:T(8,128)(2,1)S(1)}, bf16[1,64,512]{2,1,0:T(8,128)(2,1)}, u32[]{:S(2)}) copy-start(bf16[1,64,512]{2,1,0:T(8,128)(2,1)} %copy.228) | copy-start | bytes 196612
  140.2 9.5 %copy-start.74 = (bf16[1,64,512]{2,1,0:T(8,128)(2,1)S(1)}, bf16[1,64,512]{2,1,0:T(8,128)(2,1)}, u32[]{:S(2)}) copy-start(bf16[1,64,512]{2,1,0:T(8,128)(2,1)} %copy.226) | copy-start | bytes 196612
  140.2 9.6 %copy-start.68 = (bf16[1,64,512]{2,1,0:T(8,128)(2,1)S(1)}, bf16[1,64,512]{2,1,0:T(8,128)(2,1)}, u32[]{:S(2)}) copy-start(bf16[1,64,512]{2,1,0:T(8,128)(2,1)} %copy.229) | copy-start | bytes 196612
  141.0 8.8 %copy-start.76 = (bf16[1,64,512]{2,1,0:T(8,128)(2,1)S(1)}, bf16[1,64,512]{2,1,0:T(8,128)(2,1)}, u32[]{:S(2)}) copy-start(bf16[1,64,512]{2,1,0:T(8,128)(2,1)} %copy.225) | copy-start | bytes 196612
  161.4 12.7 %copy-start.134 = (bf16[128,8]{0,1:T(8,128)(2,1)S(1)}, bf16[128,8]{0,1:T(8,128)(2,1)}, u32[]{:S(2)}) copy-start(bf16[128,8]{0,1:T(8,128)(2,1)} %get-tuple-element.174) | copy-start | bytes 6148
  161.4 13.9 %copy-start.135 = (bf16[128,8]{0,1:T(8,128)(2,1)S(1)}, bf16[128,8]{0,1:T(8,128)(2,1)}, u32[]{:S(2)}) copy-start(bf16[128,8]{0,1:T(8,128)(2,1)} %get-tuple-element.172) | copy-start | bytes 6148
  161.4 15.1 %copy-start.110 = (bf16[128,1,8,8]{0,3,2,1:T(8,128)(2,1)S(1)}, bf16[128,1,8,8]{0,3,2,1:T(8,128)(2,1)}, u32[]{:S(2)}) copy-start(bf16[128,1,8,8]{0,3,2,1:T(8,128)(2,1)} %get-tuple-element.153) | copy-start | bytes 49156
  161.4 15.1 %copy-start.118 = (bf16[128,1,8,1]{0,3,2,1:T(2,128)(2,1)S(1)}, bf16[128,1,8,1]{0,3,2,1:T(2,128)(2,1)}, u32[]{:S(2)}) copy-start(bf16[128,1,8,1]{0,3,2,1:T(2,128)(2,1)} %copy.241) | copy-start | bytes 6148
  161.4 15.1 %copy-start.119 = (bf16[128,1,8,1]{0,3,2,1:T(2,128)(2,1)S(1)}, bf16[128,1,8,1]{0,3,2,1:T(2,128)(2,1)}, u32[]{:S(2)}) copy-start(bf16[128,1,8,1]{0,3,2,1:T(2,128)(2,1)} %copy.240) | copy-start | bytes 6148
  161.4 15.1 %copy-start.126 = (bf16[128,1,1,8]{0,3,2,1:T(8,128)(2,1)S(1)}, bf16[128,1,1,8]{0,3,2,1:T(8,128)(2,1)}, u32[]{:S(2)}) copy-start(bf16[128,1,1,8]{0,3,2,1:T(8,128)(2,1)} %get-tuple-element.169) | copy-start | bytes 6148
  161.4 15.1 %copy-start.127 = (bf16[128,1,1,8]{0,3,2,1:T(8,128)(2,1)S(1)}, bf16[128,1,1,8]{0,3,2,1:T(8,128)(2,1)}, u32[]{:S(2)}) copy-start(bf16[128,1,1,8]{0,3,2,1:T(8,128)(2,1)} %get-tuple-element.170) | copy-start | bytes 6148
  196.2 17.3 %copy-start.10 = (bf16[1,64,512]{2,1,0:T(8,128)(2,1)S(1)}, bf16[1,64,512]{2,1,0:T(8,128)(2,1)}, u32[]{:S(2)}) copy-start(bf16[1,64,512]{2,1,0:T(8,128)(2,1)} %copy.259) | copy-start | bytes 196612
  201.8 11.7 %copy-start.12 = (bf16[1,64,512]{2,1,0:T(8,128)(2,1)S(1)}, bf16[1,64,512]{2,1,0:T(8,128)(2,1)}, u32[]{:S(2)}) copy-start(bf16[1,64,512]{2,1,0:T(8,128)(2,1)} %copy.257) | copy-start | bytes 196612
  201.8 11.7 %copy-start.11 = (bf16[1,64,512]{2,1,0:T(8,128)(2,1)S(1)}, bf16[1,64,512]{2,1,0:T(8,128)(2,1)}, u32[]{:S(2)}) copy-start(bf16[1,64,512]{2,1,0:T(8,128)(2,1)} %copy.258) | copy-start | bytes 196612
  202.5 10.9 %copy-start.14 = (bf16[1,64,512]{2,1,0:T(8,128)(2,1)S(1)}, bf16[1,64,512]{2,1,0:T(8,128)(2,1)}, u32[]{:S(2)}) copy-start(bf16[1,64,512]{2,1,0:T(8,128)(2,1)} %copy.254) | copy-start | bytes 196612
  202.5 10.9 %copy-start.13 = (bf16[1,64,512]{2,1,0:T(8,128)(2,1)S(1)}, bf16[1,64,512]{2,1,0:T(8,128)(2,1)}, u32[]{:S(2)}) copy-start(bf16[1,64,512]{2,1,0:T(8,128)(2,1)} %copy.256) | copy-start | bytes 196612
  203.3 10.2 %copy-start.15 = (bf16[1,64,512]{2,1,0:T(8,128)(2,1)S(1)}, bf16[1,64,512]{2,1,0:T(8,128)(2,1)}, u32[]{:S(2)}) copy-start(bf16[1,64,512]{2,1,0:T(8,128)(2,1)} %copy.255) | copy-start | bytes 196612
  203.3 10.5 %copy-start.69 = (bf16[1,64,512]{2,1,0:T(8,128)(2,1)S(1)}, bf16[1,64,512]{2,1,0:T(8,128)(2,1)}, u32[]{:S(2)}) copy-start(bf16[1,64,512]{2,1,0:T(8,128)(2,1)} %copy.268) | copy-start | bytes 196612
  204.0 9.5 %copy-start.85 = (bf16[1,64,512]{2,1,0:T(8,128)(2,1)S(1)}, bf16[1,64,512]{2,1,0:T(8,128)(2,1)}, u32[]{:S(2)}) copy-start(bf16[1,64,512]{2,1,0:T(8,128)(2,1)} %copy.260) | copy-start | bytes 196612
  204.0 9.6 %copy-start.83 = (bf16[1,64,512]{2,1,0:T(8,128)(2,1)S(1)}, bf16[1,64,512]{2,1,0:T(8,128)(2,1)}, u32[]{:S(2)}) copy-start(bf16[1,64,512]{2,1,0:T(8,128)(2,1)} %copy.261) | copy-start | bytes 196612
  204.0 9.6 %copy-start.81 = (bf16[1,64,512]{2,1,0:T(8,128)(2,1)S(1)}, bf16[1,64,512]{2,1,0:T(8,128)(2,1)}, u32[]{:S(2)}) copy-start(bf16[1,64,512]{2,1,0:T(8,128)(2,1)} %copy.262) | copy-start | bytes 196612
  204.0 9.6 %copy-start.79 = (bf16[1,64,512]{2,1,0:T(8,128)(2,1)S(1)}, bf16[1,64,512]{2,1,0:T(8,128)(2,1)}, u32[]{:S(2)}) copy-start(bf16[1,64,512]{2,1,0:T(8,128)(2,1)} %copy.263) | copy-start | bytes 196612
  204.0 9.6 %copy-start.77 = (bf16[1,64,512]{2,1,0:T(8,128)(2,1)S(1)}, bf16[1,64,512]{2,1,0:T(8,128)(2,1)}, u32[]{:S(2)}) copy-start(bf16[1,64,512]{2,1,0:T(8,128)(2,1)} %copy.264) | copy-start | bytes 196612
  204.0 9.7 %copy-start.75 = (bf16[1,64,512]{2,1,0:T(8,128)(2,1)S(1)}, bf16[1,64,512]{2,1,0:T(8,128)(2,1)}, u32[]{:S(2)}) copy-start(bf16[1,64,512]{2,1,0:T(8,128)(2,1)} %copy.265) | copy-start | bytes 196612
  204.0 9.7 %copy-start.73 = (bf16[1,64,512]{2,1,0:T(8,128)(2,1)S(1)}, bf16[1,64,512]{2,1,0:T(8,128)(2,1)}, u32[]{:S(2)}) copy-start(bf16[1,64,512]{2,1,0:T(8,128)(2,1)} %copy.266) | copy-start | bytes 196612
  204.0 9.7 %copy-start.71 = (bf16[1,64,512]{2,1,0:T(8,128)(2,1)S(1)}, bf16[1,64,512]{2,1,0:T(8,128)(2,1)}, u32[]{:S(2)}) copy-start(bf16[1,64,512]{2,1,0:T(8,128)(2,1)} %copy.267) | copy-start | bytes 196612
  (80 other events, 190.8 us)
Sparse Core Ops, SparseCore 0:
  215.4 126.0 all-reduce.1
where the time goes:
time: 354 us; the launch traced here: 351 us
  local copies, waits for them, and re-layouts  145 us (41%)
  waiting for transfers between devices  122 us (34%)
  other arithmetic  49.6 us (14%)
  between operations  16.8 us (5%)
  starting transfers between devices  12.3 us (3%)
  matrix products  5.18 us (1%)
    psum x1, waiting for transfers between devices, per_device(): total = lax.psum(local_terms, ('slab', 'brick'))  122 us
    another operation x112, local copies, waits for them, and re-layouts, windows(): return jnp.stack(pieces, 0).reshape(27 * channels, EDGE * EDGE * EDGE)  106 us
    mul x34, other arithmetic, piece(): return block * present[slot, offset]  41.1 us
    unnamed x386, local copies, waits for them, and re-layouts  24 us
    ppermute x2, starting transfers between devices, extended(): lax.ppermute(lax.slice_in_dim(block, block.shape[dim] - width, None, axis...  8.19 us
  transfers between devices with their start and end apart: 5, of which 1 were waited for; matrix products, arithmetic and copies ran while one was open for 9% of the time, Pallas kernels for 0%

commit v1 on v0

--- a/solution.py
+++ b/solution.py
@@ -135,7 +135,7 @@
         grad_patches = windows(padded[channels:], -1)
         grad_rows = jnp.dot(backward_matrix, grad_patches, preferred_element_type=jnp.float32)
         gradients.append((grad_rows * scaling).astype(jnp.bfloat16))
-    total = lax.psum(local_terms, ("slab", "brick"))
+    total = lax.psum(lax.psum(local_terms, "brick"), "slab")
     slot_count = slots * lax.axis_size("slab") * lax.axis_size("brick")
     grad_weight = jnp.transpose(total.reshape(channels, 27, channels), (1, 0, 2)) / math.sqrt(
         voxels * slot_count

time: 354 us -> 381 us (1.076)
  local copies, waits for them, and re-layouts: 145 us -> 177 us
  waiting for transfers between devices: 122 us -> 113 us
    unnamed x386 -> x362, local copies, waits for them, and re-layouts: 24 us -> 40.6 us
    another operation x112, local copies, waits for them, and re-layouts: 106 us -> 121 us  [windows(): return jnp.stack(pieces, 0).reshape(27 * channels, EDGE * EDGE * EDGE)]
    psum x1 -> x2, waiting for transfers between devices: 122 us -> 113 us  [per_device(): total = lax.psum(lax.psum(local_terms, 'brick'), 'slab')]
  transfers between devices with their start and end apart: 5 -> 6, of which waited for: 1 -> 2; matrix products, arithmetic and copies ran while one was open for 9% -> 8% of each run, Pallas kernels for 0% -> 0%
where the time goes in v1:
time: 381 us; the launch traced here: 377 us
  local copies, waits for them, and re-layouts  177 us (46%)
  waiting for transfers between devices  113 us (30%)
  other arithmetic  52.7 us (14%)
  between operations  16.7 us (4%)
  starting transfers between devices  12.4 us (3%)
  matrix products  5.37 us (1%)
    another operation x112, local copies, waits for them, and re-layouts, windows(): return jnp.stack(pieces, 0).reshape(27 * channels, EDGE * EDGE * EDGE)  121 us
    psum x2, waiting for transfers between devices, per_device(): total = lax.psum(lax.psum(local_terms, 'brick'), 'slab')  113 us
    mul x34, other arithmetic, piece(): return block * present[slot, offset]  42.5 us
    unnamed x362, local copies, waits for them, and re-layouts  40.6 us
    ppermute x2, starting transfers between devices, extended(): lax.ppermute(lax.slice_in_dim(block, block.shape[dim] - width, None, axis...  8.19 us
    slice x8, local copies, waits for them, and re-layouts, windows(): padded[:, begin_z:begin_z + EDGE, begin_y:begin_y + EDGE, begin_x:begin_x...  7.82 us
  transfers between devices with their start and end apart: 6, of which 2 were waited for; matrix products, arithmetic and copies ran while one was open for 8% of the time, Pallas kernels for 0%

profile of v1, /device:TPU:1, one launch (start us, length us, event | category | flops | bytes accessed | tf_op | source)
XLA Modules:
  0.0 377.2 jit_solution(1540210900237812551)
XLA Ops:
  12.2 4.0 %collective-permute-start = (bf16[1,1,6,128,64]{3,4,2,1,0:T(8,128)(2,1)S(1)}, bf16[1,1,6,128,64]{3,4,2,1,0:T(8,128)(2,1)S(1)}, u32[]{:S(2)}, u32[]{:S(2)}) collective-permute-start(bf16[1,1,6,128,64]{3,4,2,1,0:T(8,128)(2,1)S(1)} %maximum_bitcast_fusion), channel_id=1, source_target_pairs={{0,16},{1,17},{2,18},{3,19},{4,20},{5,21},{6,22},{7,23},{8,24},{9,... | collective-permute-start | bytes 294920 | tf_op jit(solution)/shard_map/ppermute | solution.py:15
  22.9 1.9 slice_multiply_fusion.19
  27.2 1.8 slice_multiply_fusion.15
  29.1 2.8 collective-permute-start.3
  31.9 4.2 %collective-permute-start.2 = (bf16[3,1,6,128,64]{3,4,2,1,0:T(8,128)(2,1)S(1)}, bf16[3,1,6,128,64]{3,4,2,1,0:T(8,128)(2,1)S(1)}, u32[]{:S(2)}, u32[]{:S(2)}) collective-permute-start(bf16[3,1,6,128,64]{3,4,2,1,0:T(8,128)(2,1)S(1)} %pad_maximum_fusion), channel_id=1, source_target_pairs={{0,1},{1,2},{2,3},{3,4},{4,5},{5,6},{6,7},{7,8},{8,9},{9,10},{10,1... | collective-permute-start | bytes 884744 | tf_op jit(solution)/shard_map/ppermute | solution.py:15
  38.6 1.8 fusion.28
  40.4 1.7 fusion.34
  69.6 1.6 copy.308
  71.2 1.6 copy.307
  72.8 1.6 copy.306
  74.4 1.6 copy.259
  99.6 1.6 copy.295
  101.2 1.6 copy.294
  102.8 1.6 copy.293
  114.7 2.0 fusion.45
  116.6 1.9 fusion.46
  121.1 1.6 copy.277
  122.7 1.6 copy.276
  124.3 1.6 copy.275
  126.0 1.6 copy.274
  127.6 1.6 copy.273
  129.2 1.6 copy.272
  130.8 1.6 copy.271
  132.4 1.6 copy.270
  134.1 1.6 copy.269
  137.3 1.6 copy.228
  138.9 1.6 copy.227
  155.2 1.9 fusion.41
  157.1 2.1 fusion.42
  159.5 1.7 fusion.49
  161.2 1.6 copy.323
  162.9 1.6 copy.322
  164.5 1.6 copy.321
  166.1 1.6 copy.320
  167.7 1.6 copy.319
  169.3 1.6 copy.318
  170.9 1.6 copy.317
  172.6 1.6 copy.316
  174.2 1.6 copy.315
  175.8 1.6 copy.250
  177.4 1.6 copy.249
  179.0 1.6 copy.248
  180.6 1.6 copy.247
  182.3 1.6 copy.246
  183.9 1.6 copy.245
  187.7 1.9 multiply_bitcast_fusion.12
  189.6 2.0 multiply_bitcast_fusion.13
  192.6 1.7 fusion.50
  194.3 1.6 copy.305
  197.5 1.6 copy.303
  199.1 1.6 copy.302
  200.7 1.6 copy.301
  202.3 1.6 copy.300
  203.9 1.6 copy.299
  205.5 1.6 copy.298
  207.2 1.6 copy.297
  208.8 1.6 copy.268
  210.4 1.6 copy.267
  212.0 1.6 copy.266
  213.7 1.6 copy.265
  215.3 1.6 copy.264
  245.7 2.9 convolution_add_fusion
  253.6 84.5 %all-reduce.3.cloned.1.call-done = f32[64,1728]{1,0:T(8,128)} async-done(((f32[64,1728]{1,0:T(8,128)}), f32[64,1728]{1,0:T(8,128)}) %all-reduce.3.cloned.1.call-update) | async-done | bytes 442384 | tf_op jit(solution)/shard_map/psum | solution.py:138
  339.3 28.2 %all-reduce.5.cloned.1.call-done = f32[64,1728]{1,0:T(8,128)} async-done(((f32[64,1728]{1,0:T(8,128)}), f32[64,1728]{1,0:T(8,128)}) %all-reduce.5.cloned.1.call-update) | async-done | bytes 442384 | tf_op jit(solution)/shard_map/psum | solution.py:138
  (522 shorter events, 137.2 us)
Async XLA Ops:
  7.2 241.5 %copy-start = (bf16[27,64,64]{2,1,0:T(8,128)(2,1)S(1)}, bf16[27,64,64]{2,1,0:T(8,128)(2,1)}, u32[]{:S(2)}) copy-start(bf16[27,64,64]{2,1,0:T(8,128)(2,1)} %param.6) | copy-start | bytes 663556
  7.2 9.0 %copy-start.126 = (s32[2,27]{1,0:T(2,128)S(1)}, s32[2,27]{1,0:T(2,128)}, u32[]{:S(2)}) copy-start(s32[2,27]{1,0:T(2,128)} %param.9) | copy-start | bytes 652
  7.2 330.9 %all-reduce.3.cloned.1.call-start = ((), (), s32[]{:S(2)}) async-start(), calls=%async_computation | async-start | bytes 917504 | tf_op jit(solution)/shard_map/psum | solution.py:138
  10.9 18.1 %collective-permute-start.1 = (bf16[1,1,6,128,64]{3,4,2,1,0:T(8,128)(2,1)S(1)}, bf16[1,1,6,128,64]{3,4,2,1,0:T(8,128)(2,1)S(1)}, u32[]{:S(2)}, u32[]{:S(2)}) collective-permute-start(bf16[1,1,6,128,64]{3,4,2,1,0:T(8,128)(2,1)S(1)} %maximum_bitcast_fusion), channel_id=1, source_target_pairs={{16,0},{17,1},{18,2},{19,3},{20,4},{21,5},{22,6},{23,7},{24,8},{25... | collective-permute-start | bytes 294920 | tf_op jit(solution)/shard_map/ppermute | solution.py:18
  12.2 16.8 %collective-permute-start = (bf16[1,1,6,128,64]{3,4,2,1,0:T(8,128)(2,1)S(1)}, bf16[1,1,6,128,64]{3,4,2,1,0:T(8,128)(2,1)S(1)}, u32[]{:S(2)}, u32[]{:S(2)}) collective-permute-start(bf16[1,1,6,128,64]{3,4,2,1,0:T(8,128)(2,1)S(1)} %maximum_bitcast_fusion), channel_id=1, source_target_pairs={{0,16},{1,17},{2,18},{3,19},{4,20},{5,21},{6,22},{7,23},{8,24},{9,... | collective-permute-start | bytes 294920 | tf_op jit(solution)/shard_map/ppermute | solution.py:15
  27.2 33.3 %copy-start.88 = (bf16[128,8,1,8]{0,3,2,1:T(8,128)(2,1)}, bf16[128,8,1,8]{0,3,2,1:T(8,128)(2,1)S(1)}, u32[]{:S(2)}) copy-start(bf16[128,8,1,8]{0,3,2,1:T(8,128)(2,1)S(1)} %get-tuple-element.145) | copy-start | bytes 49156
  27.2 33.3 %copy-start.90 = (bf16[128,8,1,8]{0,3,2,1:T(8,128)(2,1)}, bf16[128,8,1,8]{0,3,2,1:T(8,128)(2,1)S(1)}, u32[]{:S(2)}) copy-start(bf16[128,8,1,8]{0,3,2,1:T(8,128)(2,1)S(1)} %get-tuple-element.146) | copy-start | bytes 49156
  29.1 13.0 %collective-permute-start.3 = (bf16[3,1,6,128,64]{3,4,2,1,0:T(8,128)(2,1)S(1)}, bf16[3,1,6,128,64]{3,4,2,1,0:T(8,128)(2,1)S(1)}, u32[]{:S(2)}, u32[]{:S(2)}) collective-permute-start(bf16[3,1,6,128,64]{3,4,2,1,0:T(8,128)(2,1)S(1)} %pad_maximum_fusion), channel_id=1, source_target_pairs={{1,0},{2,1},{3,2},{4,3},{5,4},{6,5},{7,6},{8,7},{9,8},{10,9},{11,1... | collective-permute-start | bytes 884744 | tf_op jit(solution)/shard_map/ppermute | solution.py:18
  31.9 19.1 %collective-permute-start.2 = (bf16[3,1,6,128,64]{3,4,2,1,0:T(8,128)(2,1)S(1)}, bf16[3,1,6,128,64]{3,4,2,1,0:T(8,128)(2,1)S(1)}, u32[]{:S(2)}, u32[]{:S(2)}) collective-permute-start(bf16[3,1,6,128,64]{3,4,2,1,0:T(8,128)(2,1)S(1)} %pad_maximum_fusion), channel_id=1, source_target_pairs={{0,1},{1,2},{2,3},{3,4},{4,5},{5,6},{6,7},{7,8},{8,9},{9,10},{10,1... | collective-permute-start | bytes 884744 | tf_op jit(solution)/shard_map/ppermute | solution.py:15
  43.4 7.5 %copy-start.112 = (bf16[128,8,8]{0,2,1:T(8,128)(2,1)}, bf16[128,8,8]{0,2,1:T(8,128)(2,1)S(1)}, u32[]{:S(2)}) copy-start(bf16[128,8,8]{0,2,1:T(8,128)(2,1)S(1)} %get-tuple-element.118) | copy-start | bytes 49156
  43.5 21.7 %copy-start.114 = (bf16[128,8,8]{0,2,1:T(8,128)(2,1)}, bf16[128,8,8]{0,2,1:T(8,128)(2,1)S(1)}, u32[]{:S(2)}) copy-start(bf16[128,8,8]{0,2,1:T(8,128)(2,1)S(1)} %get-tuple-element.117) | copy-start | bytes 49156
  47.3 13.2 %copy-start.102 = (bf16[128,8,1,1]{0,3,2,1:T(2,128)(2,1)}, bf16[128,8,1,1]{0,3,2,1:T(2,128)(2,1)S(1)}, u32[]{:S(2)}) copy-start(bf16[128,8,1,1]{0,3,2,1:T(2,128)(2,1)S(1)} %copy.198) | copy-start | bytes 6148
  47.3 13.2 %copy-start.104 = (bf16[128,8,1,1]{0,3,2,1:T(2,128)(2,1)}, bf16[128,8,1,1]{0,3,2,1:T(2,128)(2,1)S(1)}, u32[]{:S(2)}) copy-start(bf16[128,8,1,1]{0,3,2,1:T(2,128)(2,1)S(1)} %copy.192) | copy-start | bytes 6148
  52.4 7.4 %copy-start.113 = (bf16[128,8,8]{0,2,1:T(8,128)(2,1)}, bf16[128,8,8]{0,2,1:T(8,128)(2,1)S(1)}, u32[]{:S(2)}) copy-start(bf16[128,8,8]{0,2,1:T(8,128)(2,1)S(1)} %get-tuple-element.112) | copy-start | bytes 49156
  52.4 14.1 %copy-start.115 = (bf16[128,8,8]{0,2,1:T(8,128)(2,1)}, bf16[128,8,8]{0,2,1:T(8,128)(2,1)S(1)}, u32[]{:S(2)}) copy-start(bf16[128,8,8]{0,2,1:T(8,128)(2,1)S(1)} %get-tuple-element.111) | copy-start | bytes 49156
  53.6 6.9 %copy-start.106 = (bf16[128,8,1,1]{0,3,2,1:T(2,128)(2,1)}, bf16[128,8,1,1]{0,3,2,1:T(2,128)(2,1)S(1)}, u32[]{:S(2)}) copy-start(bf16[128,8,1,1]{0,3,2,1:T(2,128)(2,1)S(1)} %copy.197) | copy-start | bytes 6148
  54.3 6.2 %copy-start.108 = (bf16[128,8,1,1]{0,3,2,1:T(2,128)(2,1)}, bf16[128,8,1,1]{0,3,2,1:T(2,128)(2,1)S(1)}, u32[]{:S(2)}) copy-start(bf16[128,8,1,1]{0,3,2,1:T(2,128)(2,1)S(1)} %copy.191) | copy-start | bytes 6148
  87.8 7.6 %copy-start.124 = (bf16[128,8]{0,1:T(8,128)(2,1)S(1)}, bf16[128,8]{0,1:T(8,128)(2,1)}, u32[]{:S(2)}) copy-start(bf16[128,8]{0,1:T(8,128)(2,1)} %get-tuple-element.164) | copy-start | bytes 6148
  87.8 8.8 %copy-start.125 = (bf16[128,8]{0,1:T(8,128)(2,1)S(1)}, bf16[128,8]{0,1:T(8,128)(2,1)}, u32[]{:S(2)}) copy-start(bf16[128,8]{0,1:T(8,128)(2,1)} %get-tuple-element.162) | copy-start | bytes 6148
  87.8 10.1 %copy-start.89 = (bf16[128,8,1,8]{0,3,2,1:T(8,128)(2,1)S(1)}, bf16[128,8,1,8]{0,3,2,1:T(8,128)(2,1)}, u32[]{:S(2)}) copy-start(bf16[128,8,1,8]{0,3,2,1:T(8,128)(2,1)} %copy-done.88) | copy-start | bytes 49156
  87.8 10.1 %copy-start.91 = (bf16[128,8,1,8]{0,3,2,1:T(8,128)(2,1)S(1)}, bf16[128,8,1,8]{0,3,2,1:T(8,128)(2,1)}, u32[]{:S(2)}) copy-start(bf16[128,8,1,8]{0,3,2,1:T(8,128)(2,1)} %copy-done.90) | copy-start | bytes 49156
  87.8 10.1 %copy-start.103 = (bf16[128,8,1,1]{0,3,2,1:T(2,128)(2,1)S(1)}, bf16[128,8,1,1]{0,3,2,1:T(2,128)(2,1)}, u32[]{:S(2)}) copy-start(bf16[128,8,1,1]{0,3,2,1:T(2,128)(2,1)} %copy-done.102) | copy-start | bytes 6148
  87.9 10.1 %copy-start.105 = (bf16[128,8,1,1]{0,3,2,1:T(2,128)(2,1)S(1)}, bf16[128,8,1,1]{0,3,2,1:T(2,128)(2,1)}, u32[]{:S(2)}) copy-start(bf16[128,8,1,1]{0,3,2,1:T(2,128)(2,1)} %copy-done.104) | copy-start | bytes 6148
  87.9 10.1 %copy-start.107 = (bf16[128,8,1,1]{0,3,2,1:T(2,128)(2,1)S(1)}, bf16[128,8,1,1]{0,3,2,1:T(2,128)(2,1)}, u32[]{:S(2)}) copy-start(bf16[128,8,1,1]{0,3,2,1:T(2,128)(2,1)} %copy-done.106) | copy-start | bytes 6148
  87.9 10.1 %copy-start.109 = (bf16[128,8,1,1]{0,3,2,1:T(2,128)(2,1)S(1)}, bf16[128,8,1,1]{0,3,2,1:T(2,128)(2,1)}, u32[]{:S(2)}) copy-start(bf16[128,8,1,1]{0,3,2,1:T(2,128)(2,1)} %copy-done.108) | copy-start | bytes 6148
  87.9 10.1 %copy-start.110 = (bf16[128,1,8,8]{0,3,2,1:T(8,128)(2,1)S(1)}, bf16[128,1,8,8]{0,3,2,1:T(8,128)(2,1)}, u32[]{:S(2)}) copy-start(bf16[128,1,8,8]{0,3,2,1:T(8,128)(2,1)} %get-tuple-element.151) | copy-start | bytes 49156
  87.9 10.1 %copy-start.118 = (bf16[128,1,8,1]{0,3,2,1:T(2,128)(2,1)S(1)}, bf16[128,1,8,1]{0,3,2,1:T(2,128)(2,1)}, u32[]{:S(2)}) copy-start(bf16[128,1,8,1]{0,3,2,1:T(2,128)(2,1)} %copy.188) | copy-start | bytes 6148
  87.9 10.1 %copy-start.119 = (bf16[128,1,8,1]{0,3,2,1:T(2,128)(2,1)S(1)}, bf16[128,1,8,1]{0,3,2,1:T(2,128)(2,1)}, u32[]{:S(2)}) copy-start(bf16[128,1,8,1]{0,3,2,1:T(2,128)(2,1)} %copy.187) | copy-start | bytes 6148
  87.9 10.1 %copy-start.122 = (bf16[128,1,1,8]{0,3,2,1:T(8,128)(2,1)S(1)}, bf16[128,1,1,8]{0,3,2,1:T(8,128)(2,1)}, u32[]{:S(2)}) copy-start(bf16[128,1,1,8]{0,3,2,1:T(8,128)(2,1)} %get-tuple-element.159) | copy-start | bytes 6148
  87.9 10.1 %copy-start.123 = (bf16[128,1,1,8]{0,3,2,1:T(8,128)(2,1)S(1)}, bf16[128,1,1,8]{0,3,2,1:T(8,128)(2,1)}, u32[]{:S(2)}) copy-start(bf16[128,1,1,8]{0,3,2,1:T(8,128)(2,1)} %get-tuple-element.160) | copy-start | bytes 6148
  138.9 14.7 %copy-start.52 = (bf16[1,64,512]{2,1,0:T(8,128)(2,1)S(1)}, bf16[1,64,512]{2,1,0:T(8,128)(2,1)}, u32[]{:S(2)}) copy-start(bf16[1,64,512]{2,1,0:T(8,128)(2,1)} %copy.220) | copy-start | bytes 196612
  141.3 12.2 %copy-start.55 = (bf16[1,64,512]{2,1,0:T(8,128)(2,1)S(1)}, bf16[1,64,512]{2,1,0:T(8,128)(2,1)}, u32[]{:S(2)}) copy-start(bf16[1,64,512]{2,1,0:T(8,128)(2,1)} %copy.218) | copy-start | bytes 196612
  141.3 12.3 %copy-start.54 = (bf16[1,64,512]{2,1,0:T(8,128)(2,1)S(1)}, bf16[1,64,512]{2,1,0:T(8,128)(2,1)}, u32[]{:S(2)}) copy-start(bf16[1,64,512]{2,1,0:T(8,128)(2,1)} %copy.219) | copy-start | bytes 196612
  142.0 11.4 %copy-start.57 = (bf16[1,64,512]{2,1,0:T(8,128)(2,1)S(1)}, bf16[1,64,512]{2,1,0:T(8,128)(2,1)}, u32[]{:S(2)}) copy-start(bf16[1,64,512]{2,1,0:T(8,128)(2,1)} %copy.215) | copy-start | bytes 196612
  142.0 11.5 %copy-start.56 = (bf16[1,64,512]{2,1,0:T(8,128)(2,1)S(1)}, bf16[1,64,512]{2,1,0:T(8,128)(2,1)}, u32[]{:S(2)}) copy-start(bf16[1,64,512]{2,1,0:T(8,128)(2,1)} %copy.217) | copy-start | bytes 196612
  142.8 10.7 %copy-start.64 = (bf16[1,64,512]{2,1,0:T(8,128)(2,1)S(1)}, bf16[1,64,512]{2,1,0:T(8,128)(2,1)}, u32[]{:S(2)}) copy-start(bf16[1,64,512]{2,1,0:T(8,128)(2,1)} %copy.214) | copy-start | bytes 196612
  142.8 10.7 %copy-start.58 = (bf16[1,64,512]{2,1,0:T(8,128)(2,1)S(1)}, bf16[1,64,512]{2,1,0:T(8,128)(2,1)}, u32[]{:S(2)}) copy-start(bf16[1,64,512]{2,1,0:T(8,128)(2,1)} %copy.216) | copy-start | bytes 196612
  143.5 10.4 %copy-start.74 = (bf16[1,64,512]{2,1,0:T(8,128)(2,1)S(1)}, bf16[1,64,512]{2,1,0:T(8,128)(2,1)}, u32[]{:S(2)}) copy-start(bf16[1,64,512]{2,1,0:T(8,128)(2,1)} %copy.227) | copy-start | bytes 196612
  143.5 10.4 %copy-start.72 = (bf16[1,64,512]{2,1,0:T(8,128)(2,1)S(1)}, bf16[1,64,512]{2,1,0:T(8,128)(2,1)}, u32[]{:S(2)}) copy-start(bf16[1,64,512]{2,1,0:T(8,128)(2,1)} %copy.228) | copy-start | bytes 196612
  144.2 9.6 %copy-start.76 = (bf16[1,64,512]{2,1,0:T(8,128)(2,1)S(1)}, bf16[1,64,512]{2,1,0:T(8,128)(2,1)}, u32[]{:S(2)}) copy-start(bf16[1,64,512]{2,1,0:T(8,128)(2,1)} %copy.226) | copy-start | bytes 196612
  144.2 9.7 %copy-start.70 = (bf16[1,64,512]{2,1,0:T(8,128)(2,1)S(1)}, bf16[1,64,512]{2,1,0:T(8,128)(2,1)}, u32[]{:S(2)}) copy-start(bf16[1,64,512]{2,1,0:T(8,128)(2,1)} %copy.229) | copy-start | bytes 196612
  144.9 8.7 %copy-start.86 = (bf16[1,64,512]{2,1,0:T(8,128)(2,1)S(1)}, bf16[1,64,512]{2,1,0:T(8,128)(2,1)}, u32[]{:S(2)}) copy-start(bf16[1,64,512]{2,1,0:T(8,128)(2,1)} %copy.221) | copy-start | bytes 196612
  144.9 8.7 %copy-start.84 = (bf16[1,64,512]{2,1,0:T(8,128)(2,1)S(1)}, bf16[1,64,512]{2,1,0:T(8,128)(2,1)}, u32[]{:S(2)}) copy-start(bf16[1,64,512]{2,1,0:T(8,128)(2,1)} %copy.222) | copy-start | bytes 196612
  145.0 8.8 %copy-start.82 = (bf16[1,64,512]{2,1,0:T(8,128)(2,1)S(1)}, bf16[1,64,512]{2,1,0:T(8,128)(2,1)}, u32[]{:S(2)}) copy-start(bf16[1,64,512]{2,1,0:T(8,128)(2,1)} %copy.223) | copy-start | bytes 196612
  145.0 8.8 %copy-start.80 = (bf16[1,64,512]{2,1,0:T(8,128)(2,1)S(1)}, bf16[1,64,512]{2,1,0:T(8,128)(2,1)}, u32[]{:S(2)}) copy-start(bf16[1,64,512]{2,1,0:T(8,128)(2,1)} %copy.224) | copy-start | bytes 196612
  145.0 8.9 %copy-start.78 = (bf16[1,64,512]{2,1,0:T(8,128)(2,1)S(1)}, bf16[1,64,512]{2,1,0:T(8,128)(2,1)}, u32[]{:S(2)}) copy-start(bf16[1,64,512]{2,1,0:T(8,128)(2,1)} %copy.225) | copy-start | bytes 196612
  153.7 5.6 %copy-start.95 = (bf16[128,8,1,1]{0,3,2,1:T(2,128)(2,1)S(1)}, bf16[128,8,1,1]{0,3,2,1:T(2,128)(2,1)}, u32[]{:S(2)}) copy-start(bf16[128,8,1,1]{0,3,2,1:T(2,128)(2,1)} %copy-done.94) | copy-start | bytes 6148
  212.0 27.3 %copy-start.21 = (bf16[1,64,512]{2,1,0:T(8,128)(2,1)S(1)}, bf16[1,64,512]{2,1,0:T(8,128)(2,1)}, u32[]{:S(2)}) copy-start(bf16[1,64,512]{2,1,0:T(8,128)(2,1)} %copy.259) | copy-start | bytes 196612
  217.6 20.4 %copy-start.25 = (bf16[1,64,512]{2,1,0:T(8,128)(2,1)S(1)}, bf16[1,64,512]{2,1,0:T(8,128)(2,1)}, u32[]{:S(2)}) copy-start(bf16[1,64,512]{2,1,0:T(8,128)(2,1)} %copy.257) | copy-start | bytes 196612
  217.6 21.0 %copy-start.23 = (bf16[1,64,512]{2,1,0:T(8,128)(2,1)S(1)}, bf16[1,64,512]{2,1,0:T(8,128)(2,1)}, u32[]{:S(2)}) copy-start(bf16[1,64,512]{2,1,0:T(8,128)(2,1)} %copy.258) | copy-start | bytes 196612
  218.4 17.7 %copy-start.30 = (bf16[1,64,512]{2,1,0:T(8,128)(2,1)S(1)}, bf16[1,64,512]{2,1,0:T(8,128)(2,1)}, u32[]{:S(2)}) copy-start(bf16[1,64,512]{2,1,0:T(8,128)(2,1)} %copy.254) | copy-start | bytes 196612
  218.4 19.0 %copy-start.28 = (bf16[1,64,512]{2,1,0:T(8,128)(2,1)S(1)}, bf16[1,64,512]{2,1,0:T(8,128)(2,1)}, u32[]{:S(2)}) copy-start(bf16[1,64,512]{2,1,0:T(8,128)(2,1)} %copy.256) | copy-start | bytes 196612
  219.1 17.6 %copy-start.32 = (bf16[1,64,512]{2,1,0:T(8,128)(2,1)S(1)}, bf16[1,64,512]{2,1,0:T(8,128)(2,1)}, u32[]{:S(2)}) copy-start(bf16[1,64,512]{2,1,0:T(8,128)(2,1)} %copy.255) | copy-start | bytes 196612
  219.1 25.9 %copy-start.71 = (bf16[1,64,512]{2,1,0:T(8,128)(2,1)S(1)}, bf16[1,64,512]{2,1,0:T(8,128)(2,1)}, u32[]{:S(2)}) copy-start(bf16[1,64,512]{2,1,0:T(8,128)(2,1)} %copy.268) | copy-start | bytes 196612
  219.8 20.1 %copy-start.87 = (bf16[1,64,512]{2,1,0:T(8,128)(2,1)S(1)}, bf16[1,64,512]{2,1,0:T(8,128)(2,1)}, u32[]{:S(2)}) copy-start(bf16[1,64,512]{2,1,0:T(8,128)(2,1)} %copy.260) | copy-start | bytes 196612
  219.8 20.8 %copy-start.85 = (bf16[1,64,512]{2,1,0:T(8,128)(2,1)S(1)}, bf16[1,64,512]{2,1,0:T(8,128)(2,1)}, u32[]{:S(2)}) copy-start(bf16[1,64,512]{2,1,0:T(8,128)(2,1)} %copy.261) | copy-start | bytes 196612
  219.8 21.4 %copy-start.83 = (bf16[1,64,512]{2,1,0:T(8,128)(2,1)S(1)}, bf16[1,64,512]{2,1,0:T(8,128)(2,1)}, u32[]{:S(2)}) copy-start(bf16[1,64,512]{2,1,0:T(8,128)(2,1)} %copy.262) | copy-start | bytes 196612
  219.8 22.0 %copy-start.81 = (bf16[1,64,512]{2,1,0:T(8,128)(2,1)S(1)}, bf16[1,64,512]{2,1,0:T(8,128)(2,1)}, u32[]{:S(2)}) copy-start(bf16[1,64,512]{2,1,0:T(8,128)(2,1)} %copy.263) | copy-start | bytes 196612
  219.8 22.7 %copy-start.79 = (bf16[1,64,512]{2,1,0:T(8,128)(2,1)S(1)}, bf16[1,64,512]{2,1,0:T(8,128)(2,1)}, u32[]{:S(2)}) copy-start(bf16[1,64,512]{2,1,0:T(8,128)(2,1)} %copy.264) | copy-start | bytes 196612
  219.9 23.3 %copy-start.77 = (bf16[1,64,512]{2,1,0:T(8,128)(2,1)S(1)}, bf16[1,64,512]{2,1,0:T(8,128)(2,1)}, u32[]{:S(2)}) copy-start(bf16[1,64,512]{2,1,0:T(8,128)(2,1)} %copy.265) | copy-start | bytes 196612
  219.9 23.9 %copy-start.75 = (bf16[1,64,512]{2,1,0:T(8,128)(2,1)S(1)}, bf16[1,64,512]{2,1,0:T(8,128)(2,1)}, u32[]{:S(2)}) copy-start(bf16[1,64,512]{2,1,0:T(8,128)(2,1)} %copy.266) | copy-start | bytes 196612
  219.9 24.5 %copy-start.73 = (bf16[1,64,512]{2,1,0:T(8,128)(2,1)S(1)}, bf16[1,64,512]{2,1,0:T(8,128)(2,1)}, u32[]{:S(2)}) copy-start(bf16[1,64,512]{2,1,0:T(8,128)(2,1)} %copy.267) | copy-start | bytes 196612
  248.6 118.8 %all-reduce.5.cloned.1.call-start = ((), (), s32[]{:S(2)}) async-start(), calls=%async_computation.1 | async-start | bytes 917504 | tf_op jit(solution)/shard_map/psum | solution.py:138
  253.2 85.0 %copy-start.39 = (bf16[1,64,512]{2,1,0:T(8,128)(2,1)S(1)}, bf16[1,64,512]{2,1,0:T(8,128)(2,1)}, u32[]{:S(2)}) copy-start(bf16[1,64,512]{2,1,0:T(8,128)(2,1)} %copy.323) | copy-start | bytes 196612
  (69 other events, 131.2 us)
Sparse Core Ops, SparseCore 0:
  248.7 89.3 all-reduce.2
  340.4 27.0 all-reduce.4
